TPU v7x, 128 devices: a whole 4x4x4 slice. The times are simulated.
128 devices in a mesh: fsdp: 16 (over z, x), tp: 8 (over y, core).
Axes of the slice: x: 4, y: 4, z: 4, core: 2. Of those that a mesh axis runs over, the one named last changes fastest.
Arguments:
- gradient: bfloat16 [8192, 14336], P('fsdp', 'tp'), may hold values from -6 to 6
- momentum: float32 [8192, 14336], P('fsdp', 'tp'), may hold values from -18 to 18
- basis: float32 [14336, 512], P('tp'), may hold values from -0.046875 to 0.046875
Outputs:
- new_momentum: float32 [8192, 14336], P('fsdp', 'tp')
- new_basis: float32 [14336, 512], P('tp')
- update: bfloat16 [8192, 14336], P('fsdp', 'tp')
All inputs are finite; a program needn't handle non-finite values.
Results may differ from a plain program's by a relative error of at most 0.001.
Values sent between devices are 32-bit elements; how exact they have to be, the bound alone decides.
A program may use at most 128 MiB of HBM per device.

v0:
```python
import jax
import jax.numpy as jnp
from jax import lax
from jax.sharding import PartitionSpec as P

ROWS = 8192
COLS = 14336
RANK = 512


def matmul(left, right):
    return jnp.dot(left, right, precision=lax.Precision.HIGHEST, preferred_element_type=jnp.float32)


def inner(left, right):
    return lax.dot_general(
        left,
        right,
        (((0,), (0,)), ((), ())),
        precision=lax.Precision.HIGHEST,
        preferred_element_type=jnp.float32,
    )


def outer(left, right):
    return lax.dot_general(
        left,
        right,
        (((1,), (1,)), ((), ())),
        precision=lax.Precision.HIGHEST,
        preferred_element_type=jnp.float32,
    )


def orthonormal(projected, gram):
    lower = jnp.linalg.cholesky(gram)
    return jax.scipy.linalg.solve_triangular(lower, projected.T, lower=True).T


def local(gradient, momentum, basis):
    buffer = momentum + gradient.astype(jnp.float32)
    projected = lax.psum(matmul(buffer, basis), "tp")
    gram = lax.psum(inner(projected, projected), "fsdp")
    ortho = orthonormal(projected, gram)
    back = lax.psum(inner(buffer, ortho), "fsdp")
    squares = lax.psum(jnp.sum(back * back, axis=0), "tp")
    new_momentum = buffer - 0.05 * outer(ortho, back)
    new_basis = back / (jnp.sqrt(squares) + 1e-08)
    scale = jnp.sqrt(jnp.float32(ROWS * COLS / RANK))
    update = (scale * outer(ortho, new_basis)).astype(jnp.bfloat16)
    return (new_momentum, new_basis, update)


def solution(mesh):
    return jax.shard_map(
        local,
        mesh=mesh,
        in_specs=(P("fsdp", "tp"), P("fsdp", "tp"), P("tp", None)),
        out_specs=(P("fsdp", "tp"), P("tp", None), P("fsdp", "tp")),
        check_vma=False,
    )
```

profile of v0, /device:TPU:1, one launch (start us, length us, event | category | flops | bytes accessed | tf_op | source)
XLA Modules:
  0.0 490.8 jit_solution(13153587795741546322)
XLA Ops:
  7.2 10.3 %fusion.1 = f32[512,512]{1,0:T(8,128)} fusion(f32[1792,512]{1,0:T(8,128)} %param.5, f32[512,1792]{1,0:T(8,128)} %param.4, bf16[512,1792]{1,0:T(8,128)(2,1)} %param.3), kind=kOutput, calls=%fused_computation.8 | convolution fusion | flops 5638979584 | bytes 10223616 | tf_op jit(solution)/shard_map/dot_general | solution.py:12
  17.6 63.8 %all-reduce.5.cloned.1.call-done = f32[512,512]{1,0:T(8,128)} async-done(((f32[512,512]{1,0:T(8,128)}), f32[512,512]{1,0:T(8,128)}) %all-reduce.5.cloned.1.call-update) | async-done | bytes 1048592 | tf_op jit(solution)/shard_map/psum | solution.py:42
  81.4 4.4 fusion.36
  85.8 0.2 all-reduce.9.cloned.1.call-start
  86.0 86.9 %all-reduce.7.cloned.1.call-done = f32[512,512]{0,1:T(8,128)} async-done(((f32[512,512]{0,1:T(8,128)}), f32[512,512]{0,1:T(8,128)}) %all-reduce.7.cloned.1.call-update) | async-done | bytes 1048592 | tf_op jit(solution)/shard_map/psum | solution.py:43
  172.9 1.6 copy.7
  174.5 1.4 fusion.2
  176.0 11.7 %cholesky.104 = f32[128,128]{1,0:T(8,128)S(1)} custom-call(f32[128,128]{1,0:T(8,128)S(1)} %cholesky.266), custom_call_target="Cholesky" | custom-call | tf_op jit(solution)/shard_map/jit(cholesky)/cholesky | solution.py:36
  187.7 9.8 %custom-call.31 = f32[1,128,128]{1,2,0:T(8,128)S(1)} custom-call(f32[1,128,128]{2,1,0:T(8,128)S(1)} %get-tuple-element.30), custom_call_target="InvertDiagBlocksLowerTriangular" | custom-call | tf_op jit(solution)/shard_map/jit(cholesky)/cholesky | solution.py:36
  197.7 0.3 constant_dynamic-update-slice_fusion.3
  198.0 0.3 convolution_subtract_fusion.3
  198.3 11.7 %cholesky.217 = f32[128,128]{1,0:T(8,128)S(1)} custom-call(f32[128,128]{1,0:T(8,128)S(1)} %cholesky.270), custom_call_target="Cholesky" | custom-call | tf_op jit(solution)/shard_map/jit(cholesky)/cholesky | solution.py:36
  210.1 10.2 %custom-call.32 = f32[1,128,128]{1,2,0:T(8,128)S(1)} custom-call(f32[1,128,128]{2,1,0:T(8,128)S(1)} %get-tuple-element.27), custom_call_target="InvertDiagBlocksLowerTriangular" | custom-call | tf_op jit(solution)/shard_map/jit(cholesky)/cholesky | solution.py:36
  220.3 0.3 convolution_dynamic-update-slice_fusion
  220.6 0.4 convolution_subtract_fusion.4
  221.0 11.7 %cholesky.238 = f32[128,128]{1,0:T(8,128)S(1)} custom-call(f32[128,128]{1,0:T(8,128)S(1)} %cholesky.275), custom_call_target="Cholesky" | custom-call | tf_op jit(solution)/shard_map/jit(cholesky)/cholesky | solution.py:36
  232.7 0.7 compare_reduce_fusion.1
  233.4 9.8 %custom-call.33 = f32[1,128,128]{1,2,0:T(8,128)S(1)} custom-call(f32[1,128,128]{2,1,0:T(8,128)S(1)} %get-tuple-element.24), custom_call_target="InvertDiagBlocksLowerTriangular" | custom-call | tf_op jit(solution)/shard_map/jit(cholesky)/cholesky | solution.py:36
  243.4 0.4 convolution_subtract_fusion.5
  243.8 11.7 %cholesky.255 = f32[128,128]{1,0:T(8,128)S(1)} custom-call(f32[128,128]{1,0:T(8,128)S(1)} %convolution_subtract_fusion.5), custom_call_target="Cholesky" | custom-call | tf_op jit(solution)/shard_map/jit(cholesky)/cholesky | solution.py:36
  255.6 0.6 compare_reduce_fusion
  256.2 0.7 compare_reduce_fusion.2
  259.4 1.3 select_select_fusion
  260.7 14.1 %while.1 = (s32[]{:T(128)}, f32[512,512]{1,0:T(8,128)}, s32[4,2]{0,1:T(2,128)S(1)}, f32[4,128,128]{2,1,0:T(8,128)}, s32[]{:T(128)}) while((s32[]{:T(128)}, f32[512,512]{1,0:T(8,128)}, s32[4,2]{0,1:T(2,128)S(1)}, f32[4,128,128]{2,1,0:T(8,128)}, s32[]{:T(128)}) %tuple.31), condition=%wide.while_cond, body=%wide.while_body.sunk | while | flops 2 | bytes 132205 | solution.py:37
  260.8 0.6 fusion.48
  261.4 2.9 bitcast_dynamic-update-slice_fusion.2
  264.3 0.6 fusion.48
  264.9 2.9 bitcast_dynamic-update-slice_fusion.2
  267.9 0.6 fusion.48
  268.5 2.9 bitcast_dynamic-update-slice_fusion.2
  271.4 0.6 fusion.48
  272.0 2.8 bitcast_dynamic-update-slice_fusion.2
  274.9 40.1 %custom-call.34 = f32[4,128,128]{1,2,0:T(8,128)S(1)} custom-call(f32[4,128,128]{2,1,0:T(8,128)} %get-tuple-element.10), custom_call_target="InvertDiagBlocksLowerTriangular" | custom-call | tf_op jit(solution)/shard_map/jit(_solve_triangular)/triangular_solve | solution.py:37
  315.0 0.4 fusion.11
  315.5 0.2 copy-done.8
  315.7 1.9 convolution_subtract_fusion.1
  317.6 1.3 fusion.24
  318.8 1.9 convolution_subtract_fusion
  320.7 1.3 fusion.22
  322.0 2.5 convolution_subtract_fusion.2
  324.5 1.3 fusion.21
  325.8 13.9 %fusion = f32[1792,512]{1,0:T(8,128)} fusion(f32[512,1792]{1,0:T(8,128)S(1)} %copy-done, bf16[512,1792]{1,0:T(8,128)(2,1)S(1)} %copy-done.3, f32[128,512]{1,0:T(8,128)S(1)} %fusion.21, f32[128,512]{1,0:T(8,128)S(1)} %fusion.22, f32[128,512]{1,0:T(8,128)S(1)} %fusion.24, f32[128,512]{1,0:T(8,128)S(1)} %fusion.11), kind=kOutput, calls=%fused_computation.7 | convolution fusion | flops 5639766016 | bytes 10223616 | tf_op jit(solution)/shard_map/dot_general | solution.py:16
  339.7 99.5 %all-reduce.9.cloned.1.call-done = f32[1792,512]{1,0:T(8,128)} async-done(((f32[1792,512]{1,0:T(8,128)}), f32[1792,512]{1,0:T(8,128)}) %all-reduce.9.cloned.1.call-update) | async-done | bytes 3670032 | tf_op jit(solution)/shard_map/psum | solution.py:45
  439.2 2.4 multiply_reduce_fusion
  441.6 12.8 %psum.31 = f32[512]{0:T(512)S(1)} all-reduce(f32[512]{0:T(512)S(1)} %multiply_reduce_fusion), channel_id=1, replica_groups=mesh['fsdp'=16,'tp'=8] {'tp'}, use_global_device_ids=true, to_apply=%region_12.13 | all-reduce | flops 512 | bytes 4096 | tf_op jit(solution)/shard_map/psum | solution.py:46
  454.4 2.5 broadcast_divide_fusion
  457.0 13.3 %multiply_convert_fusion = bf16[512,1792]{1,0:T(8,128)(2,1)} fusion(f32[1792,512]{1,0:T(8,128)S(1)} %broadcast_divide_fusion, f32[128,512]{1,0:T(8,128)S(1)} %fusion.21, f32[128,512]{1,0:T(8,128)S(1)} %copy-done.6, f32[128,512]{1,0:T(8,128)S(1)} %fusion.24, f32[128,512]{1,0:T(8,128)S(1)} %fusion.11), kind=kOutput, calls=%fused_computation.2 | convolution fusion | flops 5639766016 | bytes 6553600 | tf_op jit(solution)/shard_map/dot_general | solution.py:26
  470.4 13.7 %multiply_subtract_fusion = f32[512,1792]{1,0:T(8,128)} fusion(f32[1792,512]{1,0:T(8,128)S(1)} %copy-done.2, f32[512,1792]{1,0:T(8,128)S(1)} %copy-done.1, bf16[512,1792]{1,0:T(8,128)(2,1)S(1)} %copy-done.3, f32[128,512]{1,0:T(8,128)S(1)} %fusion.21, f32[128,512]{1,0:T(8,128)S(1)} %copy-done.6, f32[128,512]{1,0:T(8,128)S(1)} %fusion.24, ...), kind=kOutput, calls=%fused_computation.4 | convolution fusion | flops 5641601024 | bytes 13893632 | tf_op jit(solution)/shard_map/dot_general | solution.py:26
  (39 shorter events, 1.0 us)
Async XLA Ops:
  7.2 74.2 %all-reduce.5.cloned.1.call-start = ((), (), s32[]{:S(2)}) async-start(), calls=%async_computation | async-start | bytes 2097152 | tf_op jit(solution)/shard_map/psum | solution.py:42
  17.6 155.4 %all-reduce.7.cloned.1.call-start = ((), (), s32[]{:S(2)}) async-start(), calls=%async_computation.1 | async-start | bytes 2097152 | tf_op jit(solution)/shard_map/psum | solution.py:43
  85.8 353.4 %all-reduce.9.cloned.1.call-start = ((), (), s32[]{:S(2)}) async-start(), calls=%async_computation.2 | async-start | bytes 7340032 | tf_op jit(solution)/shard_map/psum | solution.py:45
  197.5 117.5 %copy-start.4 = (f32[512,512]{1,0:T(8,128)S(1)}, f32[512,512]{1,0:T(8,128)}, u32[]{:S(2)}) copy-start(f32[512,512]{1,0:T(8,128)} %all-reduce.5.cloned.1.call-done) | copy-start | bytes 3145732
  260.7 65.1 %copy-start.3 = (bf16[512,1792]{1,0:T(8,128)(2,1)S(1)}, bf16[512,1792]{1,0:T(8,128)(2,1)}, u32[]{:S(2)}) copy-start(bf16[512,1792]{1,0:T(8,128)(2,1)} %param.3) | copy-start | bytes 5505028
  315.0 0.7 copy-start.8
  315.0 10.8 %copy-start = (f32[512,1792]{1,0:T(8,128)S(1)}, f32[512,1792]{1,0:T(8,128)}, u32[]{:S(2)}) copy-start(f32[512,1792]{1,0:T(8,128)} %param.4) | copy-start | bytes 11010052
  322.0 3.8 copy-start.5
  454.4 2.6 copy-start.6
  457.0 13.4 %copy-start.7 = (f32[1792,512]{1,0:T(8,128)}, f32[1792,512]{1,0:T(8,128)S(1)}, u32[]{:S(2)}) copy-start(f32[1792,512]{1,0:T(8,128)S(1)} %broadcast_divide_fusion) | copy-start | bytes 11010052
  457.0 13.4 %copy-start.1 = (f32[512,1792]{1,0:T(8,128)S(1)}, f32[512,1792]{1,0:T(8,128)}, u32[]{:S(2)}) copy-start(f32[512,1792]{1,0:T(8,128)} %param.4) | copy-start | bytes 11010052
  457.0 13.4 %copy-start.2 = (f32[1792,512]{1,0:T(8,128)S(1)}, f32[1792,512]{1,0:T(8,128)}, u32[]{:S(2)}) copy-start(f32[1792,512]{1,0:T(8,128)} %all-reduce.9.cloned.1.call-done) | copy-start | bytes 11010052
Sparse Core Ops, SparseCore 0:
  17.7 63.6 all-reduce.4
  85.9 86.9 all-reduce.6
  339.8 99.3 all-reduce.8
where the time goes:
time: 497 us; the launch traced here: 491 us
  waiting for transfers between devices  250 us (50%)
  other arithmetic  127 us (26%)
  matrix products  68 us (14%)
  between operations  16.8 us (3%)
  local copies, waits for them, and re-layouts  16.1 us (3%)
  blocking collectives  12.8 us (3%)
    psum x1, waiting for transfers between devices, local(): back = lax.psum(inner(buffer, ortho), 'fsdp')  99.5 us
    psum x1, waiting for transfers between devices, local(): gram = lax.psum(inner(projected, projected), 'fsdp')  86.9 us
    another operation x14, other arithmetic, orthonormal(): lower = jnp.linalg.cholesky(gram)  78.8 us
    psum x1, waiting for transfers between devices, local(): projected = lax.psum(matmul(buffer, basis), 'tp')  63.8 us
    another operation x3, other arithmetic, orthonormal(): return jax.scipy.linalg.solve_triangular(lower, projected.T, lower=True).T  41.4 us
    dot_general x2, matrix products, outer(): lax.dot_general(left, right, (((1,), (1,)), ((), ())), precision=lax.Prec...  27 us
    dot_general x2, matrix products, inner(): lax.dot_general(left, right, (((0,), (0,)), ((), ())), precision=lax.Prec...  18.3 us
    another operation x12, local copies, waits for them, and re-layouts  14.1 us
  transfers between devices with their start and end apart: 3, of which 3 were waited for; matrix products, arithmetic and copies ran while one was open for 0% of the time, Pallas kernels for 0%

commit v1 on v0

v1 whole, which is shorter than its diff:
```python
import functools

import jax
import jax.numpy as jnp
from jax import lax
from jax.experimental import pallas as pl
from jax.experimental.pallas import tpu as pltpu
from jax.sharding import PartitionSpec as P

ROWS = 8192
COLS = 14336
RANK = 512
ROW = 512
COL = 1792
HALF = 256
CHUNK = 256
CHUNKS = COL // CHUNK
MESH = pl.DeviceIdType.MESH
HIGHEST = lax.Precision.HIGHEST
f32 = jnp.float32
bf16 = jnp.bfloat16


def split(value):
    high = value.astype(bf16)
    return high, (value - high.astype(f32)).astype(bf16)


def dot(left, right, dims=((1,), (0,)), precision=None):
    return lax.dot_general(left, right, (dims, ((), ())), precision=precision, preferred_element_type=f32)


def dot3(left, right, dims=((1,), (0,))):
    (lh, ll), (rh, rl) = left, right
    return dot(lh, rh, dims) + (dot(lh, rl, dims) + dot(ll, rh, dims))


def lanes(value, index):
    return jnp.take_along_axis(value, index, axis=1, mode="promise_in_bounds")


def factor128(tile, cols):
    sub = lax.broadcasted_iota(jnp.int32, (8, 128), 0)

    def row(ref, r, first):
        return jnp.broadcast_to(ref[r : r + 1, first : first + 128], (8, 128))

    for s in range(16):
        top = 8 * s
        block = tile[top : top + 8, 0:128]
        for j in range(8):
            cols[8 * j : 8 * j + 8, :] = lanes(block, jnp.full((8, 128), top + j, jnp.int32))
        d = {(i, j): row(cols, 8 * j + i, 0) for j in range(8) for i in range(j, 8)}
        ra = [row(tile, top + i, 0) for i in range(8)]
        re = [row(tile, top + i, 128) for i in range(8)]
        for j in range(8):
            inverse = lax.rsqrt(d[j, j])
            l = {i: d[i, j] * inverse for i in range(j + 1, 8)}
            for k in range(j + 1, 8):
                for i in range(k, 8):
                    d[i, k] = d[i, k] - l[i] * l[k]
            ra[j] = ra[j] * inverse
            re[j] = re[j] * inverse
            for i in range(j + 1, 8):
                ra[i] = ra[i] - l[i] * ra[j]
                re[i] = re[i] - l[i] * re[j]
        for i in range(8):
            tile[top + i : top + i + 1, 0:128] = ra[i][0:1]
            tile[top + i : top + i + 1, 128:256] = re[i][0:1]
        for t in range(s + 1, 16):
            at = slice(8 * t, 8 * t + 8)
            xa = tile[at, 0:128]
            xe = tile[at, 128:256]
            for k in range(8):
                c = lanes(ra[k], sub + 8 * t)
                xa = xa - c * ra[k]
                xe = xe - c * re[k]
            tile[at, 0:128] = xa
            tile[at, 128:256] = xe


def eye(n):
    return (lax.broadcasted_iota(jnp.int32, (n, n), 0) == lax.broadcasted_iota(jnp.int32, (n, n), 1)).astype(f32)


def factor_step(b, mat, tile, cols):
    n = 128
    lo, hi = b * n, b * n + n
    tile[:, 0:n] = mat[lo:hi, lo:hi]
    tile[:, n : 2 * n] = eye(n)
    factor128(tile, cols)
    mat[lo:hi, lo:hi] = eye(n)
    mat[lo:hi, :] = dot(tile[:, n : 2 * n], mat[lo:hi, :], precision=HIGHEST)
    if hi < RANK:
        mat[hi:, lo:hi] = jnp.zeros((RANK - hi, n), f32)
        mat[hi:, :] = mat[hi:, :] - dot(mat[lo:hi, hi:], mat[lo:hi, :], ((0,), (0,)), HIGHEST)


class Copies:
    def __init__(self, send, recv):
        self.send, self.recv, self.n, self.all = send, recv, 0, []

    def new(self, src, dst, device):
        i = self.n
        self.n += 1
        copy = pltpu.make_async_remote_copy(
            src_ref=src,
            dst_ref=dst,
            send_sem=self.send.at[i],
            recv_sem=self.recv.at[i],
            device_id=device,
            device_id_type=MESH,
        )
        copy.start()
        self.all.append(copy)
        return copy

    def finish(self):
        for copy in self.all:
            copy.wait_send()


class Ring:
    def __init__(self, copies, pos, right, left):
        self.copies, self.pos, self.right, self.left = copies, pos, right, left

    def at(self, base, size, step, half):
        offset = base + lax.rem(self.pos + step, 4) * size + half * (size // 2)
        return pl.ds(pl.multiple_of(offset, 8), size // 2)

    def reduce_start(self, ref, base, size, slots):
        new = self.copies.new
        self.ref, self.base, self.size, self.slots = ref, base, size, slots
        at = lambda step, half: ref.at[self.at(base, size, step, half)]
        self.r = [None] * 6
        self.r[0] = new(at(2, 0), slots.at[0], self.right)
        self.r[3] = new(at(2, 1), slots.at[3], self.left)

    def reduce_plain(self):
        new, ref, slots = self.copies.new, self.ref, self.slots
        at = lambda step, half: ref.at[self.at(self.base, self.size, step, half)]
        self.r[1] = new(at(1, 1), slots.at[1], self.right)
        self.r[4] = new(at(3, 0), slots.at[4], self.left)

    def reduce_middle(self):
        new, ref, slots = self.copies.new, self.ref, self.slots
        one = self.at(self.base, self.size, 1, 0)
        two = self.at(self.base, self.size, 3, 1)
        self.r[0].wait_recv()
        ref[one, :] = ref[one, :] + slots[0]
        self.r[2] = new(ref.at[one], slots.at[2], self.right)
        self.r[3].wait_recv()
        ref[two, :] = ref[two, :] + slots[3]
        self.r[5] = new(ref.at[two], slots.at[5], self.left)

    def reduce_end(self, out):
        ref, slots = self.ref, self.slots
        one = self.at(self.base, self.size, 0, 0)
        two = self.at(self.base, self.size, 0, 1)
        self.r[4].wait_recv()
        self.r[2].wait_recv()
        out[one, :] = ref[one, :] + slots[4] + slots[2]
        self.r[1].wait_recv()
        self.r[5].wait_recv()
        out[two, :] = ref[two, :] + slots[1] + slots[5]

    def gather_start(self, ref, base, size):
        new = self.copies.new
        self.gref, self.gbase, self.gsize = ref, base, size
        one = ref.at[self.at(base, size, 0, 0)]
        two = ref.at[self.at(base, size, 0, 1)]
        self.g = [None] * 6
        self.g[0] = new(one, one, self.right)
        self.g[2] = new(two, two, self.left)
        self.g[1] = new(two, two, self.right)
        self.g[3] = new(one, one, self.left)

    def gather_middle(self):
        new, ref = self.copies.new, self.gref
        one = ref.at[self.at(self.gbase, self.gsize, 3, 0)]
        two = ref.at[self.at(self.gbase, self.gsize, 1, 1)]
        self.g[0].wait_recv()
        self.g[4] = new(one, one, self.right)
        self.g[2].wait_recv()
        self.g[5] = new(two, two, self.left)

    def gather_end(self):
        for i in (1, 3, 4, 5):
            self.g[i].wait_recv()


def power_kernel(
    grad_hbm, mom_hbm, basis_hbm,
    w_ref, uh_ref, ul_ref, inv_ref,
    grad, mom, basis, bh, bl, qh, ql, bth, btl,
    pother, pown, precv, pslots, pfull, ph, plo,
    gpart, gslots, gmat, mat, tile, cols,
    zpart, zslots1, zslots2, zfull, lh, ll, squares, sqslots,
    load_sem, send_sem, recv_sem,
):
    f, t = lax.axis_index("fsdp"), lax.axis_index("tp")
    z, x, y, c = f // 4, f % 4, t // 2, t % 2

    def zdev(step):
        return (lax.rem(z + step, 4) * 4 + x, t)

    def xdev(step):
        return (z * 4 + lax.rem(x + step, 4), t)

    def ydev(step):
        return (f, lax.rem(y + step, 4) * 2 + c)

    def tdev(step):
        return (f, lax.rem(t + step, 8))

    sibling = (f, y * 2 + 1 - c)

    barrier = pltpu.get_barrier_semaphore()
    peers = [zdev(i) for i in (1, 2, 3)] + [xdev(i) for i in (1, 2, 3)] + [tdev(i) for i in range(1, 8)]
    for peer in peers:
        pl.semaphore_signal(barrier, inc=1, device_id=peer, device_id_type=MESH)

    loads = []
    for k in range(CHUNKS):
        at = pl.ds(k * CHUNK, CHUNK)
        loads.append([
            pltpu.make_async_copy(mom_hbm.at[:, at], mom.at[:, at], load_sem.at[3 * k]),
            pltpu.make_async_copy(grad_hbm.at[:, at], grad.at[:, at], load_sem.at[3 * k + 1]),
            pltpu.make_async_copy(basis_hbm.at[at, :], basis.at[at, :], load_sem.at[3 * k + 2]),
        ])
        for load in loads[-1]:
            load.start()

    copies = Copies(send_sem, recv_sem)

    def partial(k, half):
        at = slice(k * CHUNK, k * CHUNK + CHUNK)
        columns = pl.ds(pl.multiple_of(half * HALF, HALF), HALF)
        return dot3((bh[:, at], bl[:, at]), (qh[at, columns], ql[at, columns]))

    for k in range(CHUNKS):
        at = slice(k * CHUNK, k * CHUNK + CHUNK)
        for load in loads[k]:
            load.wait()
        bh[:, at], bl[:, at] = split(mom[:, at] + grad[:, at].astype(f32))
        qh[at, :], ql[at, :] = split(basis[at, :])
        term = partial(k, 1 - c)
        pother[...] = term if k == 0 else pother[...] + term

    pl.semaphore_wait(barrier, len(peers))
    swap = copies.new(pother, precv, sibling)
    for k in range(CHUNKS):
        term = partial(k, c)
        pown[...] = term if k == 0 else pown[...] + term
    swap.wait_recv()
    pown[...] = pown[...] + precv[...]

    def transposed(k):
        at = slice(k * CHUNK, k * CHUNK + CHUNK)
        bth[at, :], btl[at, :] = split((mom[:, at] + grad[:, at].astype(f32)).T)

    yring = Ring(copies, y, ydev(1), ydev(3))
    yring.reduce_start(pown, 0, 128, pslots)
    yring.reduce_plain()
    for k in (0, 1):
        transposed(k)
    yring.reduce_middle()
    for k in (2, 3):
        transposed(k)
    mine = pfull.at[c]
    yring.reduce_end(mine)
    yring.gather_start(mine, 0, 128)
    group = lambda step: mine.at[pl.ds(pl.multiple_of(lax.rem(y + step, 4) * 128, 128), 128)]
    shared = [copies.new(group(0), group(0), sibling)]
    for k in (4, 5):
        transposed(k)
    yring.gather_middle()
    transposed(6)
    yring.gather_end()
    for step in (1, 2, 3):
        shared.append(copies.new(group(step), group(step), sibling))
    ph[c], plo[c] = split(pfull[c])
    for copy in shared:
        copy.wait_recv()
    ph[1 - c], plo[1 - c] = split(pfull[1 - c])

    gat = pl.ds(pl.multiple_of((y % 2) * 128, 128), 128)
    gl = (ph[y // 2, :, gat], plo[y // 2, :, gat])
    for half in range(2):
        g = dot3(gl, (ph[half], plo[half]), ((0,), (0,)))
        gpart[0, :, half * HALF : half * HALF + HALF] = jnp.where(c == 0, g[0:32], g[64:96])
        gpart[1, :, half * HALF : half * HALF + HALF] = jnp.where(c == 0, g[32:64], g[96:128])

    def gram_send(stage):
        first, second = (zdev, xdev) if stage == 0 else (xdev, zdev)
        sent = []
        for step in (1, 2, 3):
            sent.append(copies.new(gpart.at[2 * stage], gslots.at[stage, 0, step - 1], first(step)))
            sent.append(copies.new(gpart.at[2 * stage + 1], gslots.at[stage, 1, step - 1], second(step)))
        return sent

    def gram_sum(stage, sent):
        for copy in sent:
            copy.wait_recv()
        for part in range(2):
            own = gpart[2 * stage + part]
            total = own + gslots[stage, part, 0] + gslots[stage, part, 1] + gslots[stage, part, 2]
            if stage == 0:
                gpart[2 + part] = total
            else:
                gmat[pl.ds(pl.multiple_of(t * 64 + part * 32, 32), 32), :] = total

    sent = gram_send(0)

    zring = Ring(copies, z, zdev(1), zdev(3))
    xring = Ring(copies, x, xdev(1), xdev(3))
    rings = ((zring, xring), (xring, zring))
    first = [Ring(copies, z, zdev(1), zdev(3)), Ring(copies, x, xdev(1), xdev(3))]
    second = [Ring(copies, x, xdev(1), xdev(3)), Ring(copies, z, zdev(1), zdev(3))]
    tall = COL // 4
    short = tall // 4
    bases = [z * tall, x * tall]

    def product(half, step):
        rows = tall // 2
        start = lax.rem(first[half].pos + step, 4) * tall

        @pl.loop(0, 2)
        def _(i):
            at = pl.ds(pl.multiple_of(start + i * rows, 32), rows)
            zpart[half, at, :] = dot3((bth[at, :], btl[at, :]), (ph[half], plo[half]))

    for half in range(2):
        product(half, 2)
        first[half].reduce_start(zpart.at[half], 0, tall, zslots1.at[half])
    for half in range(2):
        product(half, 1)
        product(half, 3)
        first[half].reduce_plain()
    gram_sum(0, sent)
    sent = gram_send(1)
    for half in range(2):
        product(half, 0)
    gram_sum(1, sent)
    rows64 = lambda step: gmat.at[pl.ds(pl.multiple_of((lax.rem(y + step, 4) * 2 + c) * 64, 64), 64)]
    spread = [copies.new(rows64(0), rows64(0), ydev(i)) for i in (1, 2, 3)]
    shared = [copies.new(rows64(0), rows64(0), sibling)]
    for half in range(2):
        first[half].reduce_middle()
    for i in (1, 2, 3):
        spread[i - 1].wait_recv()
        shared.append(copies.new(rows64(4 - i), rows64(4 - i), sibling))
    for copy in shared:
        copy.wait_recv()

    mat[...] = gmat[...]
    factor_step(0, mat, tile, cols)
    for half in range(2):
        first[half].reduce_end(zpart.at[half])
        second[half].reduce_start(zpart.at[half], bases[half], short, zslots2.at[half])
        second[half].reduce_plain()
    factor_step(1, mat, tile, cols)
    for half in range(2):
        second[half].reduce_middle()
    for half in range(2):
        second[half].reduce_end(zfull.at[half])
        second[half].gather_start(zfull.at[half], bases[half], short)
    factor_step(2, mat, tile, cols)
    for half in range(2):
        second[half].gather_middle()
    for half in range(2):
        second[half].gather_end()
        first[half].gather_start(zfull.at[half], 0, tall)
    factor_step(3, mat, tile, cols)
    r = lax.broadcasted_iota(jnp.int32, (RANK, RANK), 0)
    k = lax.broadcasted_iota(jnp.int32, (RANK, RANK), 1)
    lh[...], ll[...] = split(jnp.where(r >= k, mat[...], 0.0))
    uh_ref[...], ul_ref[...] = split(
        sum(
            dot3((ph[half], plo[half]), (lh[:, half * HALF : half * HALF + HALF], ll[:, half * HALF : half * HALF + HALF]), ((1,), (1,)))
            for half in range(2)
        )
    )
    for half in range(2):
        first[half].gather_middle()
    for half in range(2):
        first[half].gather_end()

    squares[0] = jnp.zeros((8, RANK), f32)

    @pl.loop(0, CHUNKS)
    def _(i):
        at = pl.ds(pl.multiple_of(i * CHUNK, CHUNK), CHUNK)
        w = sum(
            dot3(split(zfull[half, at, :]), (lh[:, half * HALF : half * HALF + HALF], ll[:, half * HALF : half * HALF + HALF]), ((1,), (1,)))
            for half in range(2)
        )
        w_ref[at, :] = w
        squares[0] = squares[0] + jnp.sum((w * w).reshape(CHUNK // 8, 8, RANK), axis=0)

    sent = [copies.new(squares.at[0], sqslots.at[i - 1], tdev(i)) for i in range(1, 8)]
    total = squares[0]
    for i in range(7):
        sent[i].wait_recv()
        total = total + sqslots[i]
    norms = jnp.sqrt(jnp.sum(total, axis=0, keepdims=True))
    inv_ref[...] = jnp.broadcast_to(1.0 / (norms + 1e-08), (8, RANK))
    copies.finish()


COPIES = 128


def power(gradient, momentum, basis):
    vmem = lambda shape, kind=f32: pltpu.VMEM(shape, kind)
    any_spec = pl.BlockSpec(memory_space=pl.ANY)
    vmem_spec = pl.BlockSpec(memory_space=pltpu.VMEM)
    return pl.pallas_call(
        power_kernel,
        out_shape=[
            jax.ShapeDtypeStruct((COL, RANK), f32),
            jax.ShapeDtypeStruct((ROW, RANK), bf16),
            jax.ShapeDtypeStruct((ROW, RANK), bf16),
            jax.ShapeDtypeStruct((8, RANK), f32),
        ],
        in_specs=[any_spec] * 3,
        out_specs=[vmem_spec] * 4,
        scratch_shapes=[
            vmem((ROW, COL), bf16), vmem((ROW, COL)), vmem((COL, RANK)),
            vmem((ROW, COL), bf16), vmem((ROW, COL), bf16),
            vmem((COL, RANK), bf16), vmem((COL, RANK), bf16),
            vmem((COL, ROW), bf16), vmem((COL, ROW), bf16),
            vmem((ROW, HALF)), vmem((ROW, HALF)), vmem((ROW, HALF)),
            vmem((6, 64, HALF)), vmem((2, ROW, HALF)),
            vmem((2, ROW, HALF), bf16), vmem((2, ROW, HALF), bf16),
            vmem((4, 32, RANK)), vmem((2, 2, 3, 32, RANK)), vmem((RANK, RANK)), vmem((RANK, RANK)),
            vmem((128, 256)), vmem((64, 128)),
            vmem((2, COL, HALF)), vmem((2, 6, COL // 8, HALF)), vmem((2, 6, COL // 32, HALF)),
            vmem((2, COL, HALF)),
            vmem((RANK, RANK), bf16), vmem((RANK, RANK), bf16),
            vmem((1, 8, RANK)), vmem((7, 8, RANK)),
            pltpu.SemaphoreType.DMA((3 * CHUNKS,)),
            pltpu.SemaphoreType.DMA((COPIES,)),
            pltpu.SemaphoreType.DMA((COPIES,)),
        ],
        compiler_params=pltpu.CompilerParams(
            collective_id=0, has_side_effects=True, vmem_limit_bytes=60 << 20
        ),
        name="power",
    )(gradient, momentum, basis)


def apply_kernel(scale, w_ref, uh, ul, inv, mom, grad, nm_ref, nb_ref, up_ref):
    w = w_ref[...]
    nb = w * inv[0:1, :]
    nb_ref[...] = nb
    high, low = split(nb)
    u = uh[...]
    last = ((1,), (1,))
    up_ref[...] = (scale * dot3((u, ul[...]), (high, low), last)).astype(bf16)
    nm_ref[...] = (mom[...] + grad[...].astype(f32)) - 0.05 * dot(u, w.astype(bf16), last)


def apply(w, uh, ul, inv, momentum, gradient):
    scale = float((ROWS * COLS / RANK) ** 0.5)
    whole = lambda shape: pl.BlockSpec(shape, lambda i: (0, 0))
    across = pl.BlockSpec((ROW, CHUNK), lambda i: (0, i))
    down = pl.BlockSpec((CHUNK, RANK), lambda i: (i, 0))
    return pl.pallas_call(
        functools.partial(apply_kernel, scale),
        grid=(CHUNKS,),
        out_shape=[
            jax.ShapeDtypeStruct((ROW, COL), f32),
            jax.ShapeDtypeStruct((COL, RANK), f32),
            jax.ShapeDtypeStruct((ROW, COL), bf16),
        ],
        in_specs=[down, whole((ROW, RANK)), whole((ROW, RANK)), whole((8, RANK)), across, across],
        out_specs=[across, down, across],
        compiler_params=pltpu.CompilerParams(vmem_limit_bytes=60 << 20),
        name="apply",
    )(w, uh, ul, inv, momentum, gradient)


def local(gradient, momentum, basis):
    w, uh, ul, inv = power(gradient, momentum, basis)
    return tuple(apply(w, uh, ul, inv, momentum, gradient))


def solution(mesh):
    return jax.shard_map(
        local,
        mesh=mesh,
        in_specs=(P("fsdp", "tp"), P("fsdp", "tp"), P("tp", None)),
        out_specs=(P("fsdp", "tp"), P("tp", None), P("fsdp", "tp")),
        check_vma=False,
    )
```

time: 497 us -> 121 us (0.24); the launches traced: 491 us -> 121 us
  waiting for transfers between devices: 250 us -> 0 us
  other arithmetic: 127 us -> 0 us
  Pallas kernels: 0 us -> 120 us
  matrix products: 68 us -> 0 us
  between operations: 16.8 us -> 0.64 us
  local copies, waits for them, and re-layouts: 16.1 us -> 0 us
  blocking collectives: 12.8 us -> 0 us
    psum x3 -> x0, waiting for transfers between devices: 250 us -> none  [the longest x1 99.5 us: local(): back = lax.psum(inner(buffer, ortho), 'fsdp')]
    pallas_call x0 -> x2, Pallas kernels: none -> 120 us  [the longest x1 109 us: power(): pl.pallas_call(power_kernel, out_shape=[jax.ShapeDtypeStruct((COL, RANK),...]
    another operation x17 -> x0, other arithmetic: 120 us -> none  [the longest x14 78.8 us: orthonormal(): lower = jnp.linalg.cholesky(gram)]
    dot_general x5 -> x0, matrix products: 55.6 us -> none  [the longest x2 27 us: outer(): lax.dot_general(left, right, (((1,), (1,)), ((), ())), precision=lax.Prec...]
    another operation x17 -> x0, local copies, waits for them, and re-layouts: 14.3 us -> none
    psum x1 -> x0, blocking collectives: 12.8 us -> none  [local(): squares = lax.psum(jnp.sum(back * back, axis=0), 'tp')]
    another operation x13 -> x0, matrix products: 12.4 us -> none  [the longest x7 10.5 us: orthonormal(): return jax.scipy.linalg.solve_triangular(lower, projected.T, lower=True).T]
  transfers between devices with their start and end apart: 3 -> 0, of which waited for: 3 -> 0; matrix products, arithmetic and copies ran while one was open for 0% -> 0% of each run, Pallas kernels for 0% -> 0%
where the time goes in v1:
time: 121 us
  Pallas kernels  120 us (99%)
    pallas_call x1, Pallas kernels, power(): pl.pallas_call(power_kernel, out_shape=[jax.ShapeDtypeStruct((COL, RANK),...  109 us
    pallas_call x1, Pallas kernels, apply(): pl.pallas_call(functools.partial(apply_kernel, scale), grid=(CHUNKS,), ou...  11.6 us

profile of v1, /device:TPU:1, one launch (start us, length us, event | category | flops | bytes accessed | tf_op | source)
XLA Modules:
  0.0 120.9 jit_solution(2112890759484153590)
XLA Ops:
  0.6 108.7 %power.1 = (f32[1792,512]{1,0:T(8,128)}, bf16[512,512]{1,0:T(8,128)(2,1)}, bf16[512,512]{1,0:T(8,128)(2,1)}, f32[8,512]{1,0:T(8,128)}) custom-call(bf16[512,1792]{1,0:T(8,128)(2,1)} %grad.1, f32[512,1792]{1,0:T(8,128)} %mom.1, f32[1792,512]{1,0:T(8,128)} %basis_hbm.1), custom_call_target="tpu_custom_call" | custom-call | tf_op jit(solution)/shard_map/power/pallas_call | solution.py:418
  109.4 11.6 %apply.1 = (f32[512,1792]{1,0:T(8,128)}, f32[1792,512]{1,0:T(8,128)}, bf16[512,1792]{1,0:T(8,128)(2,1)}) custom-call(f32[1792,512]{1,0:T(8,128)} %get-tuple-element.7.w_ref, bf16[512,512]{1,0:T(8,128)(2,1)} %get-tuple-element.8.uh, bf16[512,512]{1,0:T(8,128)(2,1)} %get-tuple-element.9.ul, f32[8,512]{1,0:T(8,128)} %get-tuple-element.10.inv, f32[512,1792]{1,0:T(8,128)} %mom.1, ...), custom_call_target="tpu_custom_call" | custom-call | tf_op jit(solution)/shard_map/apply/pallas_call | solution.py:469

commit v2 on v0

v2 whole, which is shorter than its diff:
```python
import functools

import jax
import jax.numpy as jnp
from jax import lax
from jax.experimental import pallas as pl
from jax.experimental.pallas import tpu as pltpu
from jax.sharding import PartitionSpec as P

ROWS = 8192
COLS = 14336
RANK = 512
ROW = 512
COL = 1792
HALF = 256
CHUNK = 256
CHUNKS = COL // CHUNK
MESH = pl.DeviceIdType.MESH
HIGHEST = lax.Precision.HIGHEST
f32 = jnp.float32
bf16 = jnp.bfloat16


def split(value):
    high = value.astype(bf16)
    return high, (value - high.astype(f32)).astype(bf16)


def dot(left, right, dims=((1,), (0,)), precision=None):
    return lax.dot_general(left, right, (dims, ((), ())), precision=precision, preferred_element_type=f32)


def dot3(left, right, dims=((1,), (0,))):
    (lh, ll), (rh, rl) = left, right
    return dot(lh, rh, dims) + (dot(lh, rl, dims) + dot(ll, rh, dims))


def lanes(value, index):
    return jnp.take_along_axis(value, index, axis=1, mode="promise_in_bounds")


def factor128(tile, cols, steps):
    sub = lax.broadcasted_iota(jnp.int32, (8, 128), 0)

    def row(ref, r, first):
        return jnp.broadcast_to(ref[r : r + 1, first : first + 128], (8, 128))

    for s in steps:
        top = 8 * s
        block = tile[top : top + 8, 0:128]
        for j in range(8):
            cols[8 * j : 8 * j + 8, :] = lanes(block, jnp.full((8, 128), top + j, jnp.int32))
        d = {(i, j): row(cols, 8 * j + i, 0) for j in range(8) for i in range(j, 8)}
        ra = [row(tile, top + i, 0) for i in range(8)]
        re = [row(tile, top + i, 128) for i in range(8)]
        for j in range(8):
            inverse = lax.rsqrt(d[j, j])
            l = {i: d[i, j] * inverse for i in range(j + 1, 8)}
            for k in range(j + 1, 8):
                for i in range(k, 8):
                    d[i, k] = d[i, k] - l[i] * l[k]
            ra[j] = ra[j] * inverse
            re[j] = re[j] * inverse
            for i in range(j + 1, 8):
                ra[i] = ra[i] - l[i] * ra[j]
                re[i] = re[i] - l[i] * re[j]
        for i in range(8):
            tile[top + i : top + i + 1, 0:128] = ra[i][0:1]
            tile[top + i : top + i + 1, 128:256] = re[i][0:1]
        for t in range(s + 1, 16):
            at = slice(8 * t, 8 * t + 8)
            xa = tile[at, 0:128]
            xe = tile[at, 128:256]
            for k in range(8):
                c = lanes(ra[k], sub + 8 * t)
                xa = xa - c * ra[k]
                xe = xe - c * re[k]
            tile[at, 0:128] = xa
            tile[at, 128:256] = xe


def eye(n):
    return (lax.broadcasted_iota(jnp.int32, (n, n), 0) == lax.broadcasted_iota(jnp.int32, (n, n), 1)).astype(f32)


def factor(mat, tile, cols):
    n = 128
    for lo in range(0, RANK, n):
        hi = lo + n
        tile[:, 0:n] = mat[lo:hi, lo:hi]
        tile[:, n : 2 * n] = eye(n)
        for part in range(4):
            factor128(tile, cols, range(4 * part, 4 * part + 4))
            yield
        mat[lo:hi, lo:hi] = eye(n)
        mat[lo:hi, :] = dot(tile[:, n : 2 * n], mat[lo:hi, :], precision=HIGHEST)
        if hi < RANK:
            mat[hi:, lo:hi] = jnp.zeros((RANK - hi, n), f32)
            mat[hi:, :] = mat[hi:, :] - dot(mat[lo:hi, hi:], mat[lo:hi, :], ((0,), (0,)), HIGHEST)
        yield


class Copies:
    def __init__(self, send, recv):
        self.send, self.recv = send, recv
        self.free, self.fresh, self.n, self.all, self.drained = [], 0, 0, [], 0

    def semaphore(self):
        self.n += 1
        return self.recv.at[self.n - 1]

    def new(self, src, dst, device, recv=None):
        if self.free:
            i = self.free.pop(0)
        else:
            i = self.fresh
            self.fresh += 1
        copy = pltpu.make_async_remote_copy(
            src_ref=src,
            dst_ref=dst,
            send_sem=self.send.at[i],
            recv_sem=self.semaphore() if recv is None else recv,
            device_id=device,
            device_id_type=MESH,
        )
        copy.start()
        self.all.append((copy, i))
        return copy

    def drain(self, upto):
        for copy, i in self.all[self.drained : upto]:
            copy.wait_send()
            self.free.append(i)
        self.drained = upto

    def count(self):
        return len(self.all)


def arrive(ref, semaphore):
    pltpu.make_async_copy(ref, ref, semaphore).wait()


class Ring:
    def __init__(self, copies, pos, right, left):
        self.copies, self.pos, self.right, self.left = copies, pos, right, left

    def place(self, base, size):
        first = (size // 2 + 7) // 8 * 8

        def at(step, part):
            offset = base + lax.rem(self.pos + step, 4) * size + part * first
            return pl.ds(pl.multiple_of(offset, 8), size - first if part else first)

        return at

    def reduce_start(self, ref, base, size, slots):
        new = self.copies.new
        at = self.place(base, size)
        self.ref, self.at = ref, at
        self.slots = [slots.at[i, 0 : at(0, 1 if i in (1, 3, 5) else 0).size] for i in range(6)]
        self.r = [None] * 6
        self.rest, self.whole = self.copies.semaphore(), slots.at[0:4]
        self.r[0] = new(ref.at[at(2, 0)], self.slots[0], self.right)
        self.r[3] = new(ref.at[at(2, 1)], self.slots[3], self.left)

    def reduce_plain(self):
        new, ref, at = self.copies.new, self.ref, self.at
        self.r[1] = new(ref.at[at(1, 1)], self.slots[1], self.right, self.rest)
        self.r[4] = new(ref.at[at(3, 0)], self.slots[4], self.left, self.rest)

    def reduce_middle(self):
        new, ref, slots = self.copies.new, self.ref, self.slots
        one, two = self.at(1, 0), self.at(3, 1)
        self.r[0].wait_recv()
        ref[one, :] = ref[one, :] + slots[0][...]
        self.r[2] = new(ref.at[one], slots[2], self.right, self.rest)
        self.r[3].wait_recv()
        ref[two, :] = ref[two, :] + slots[3][...]
        self.r[5] = new(ref.at[two], slots[5], self.left, self.rest)

    def reduce_end(self, out):
        ref, slots = self.ref, self.slots
        one, two = self.at(0, 0), self.at(0, 1)
        arrive(self.whole, self.rest)
        out[one, :] = ref[one, :] + slots[4][...] + slots[2][...]
        out[two, :] = ref[two, :] + slots[1][...] + slots[5][...]

    def gather_start(self, ref, base, size):
        new = self.copies.new
        at = self.place(base, size)
        self.out, self.gat = ref, at
        one, two = ref.at[at(0, 0)], ref.at[at(0, 1)]
        self.g = [None] * 6
        self.grest, self.gwhole = self.copies.semaphore(), ref.at[pl.ds(base, 2 * size)]
        self.g[0] = new(one, one, self.right)
        self.g[2] = new(two, two, self.left)
        self.g[1] = new(two, two, self.right, self.grest)
        self.g[3] = new(one, one, self.left, self.grest)

    def gather_middle(self):
        new, ref, at = self.copies.new, self.out, self.gat
        one, two = ref.at[at(3, 0)], ref.at[at(1, 1)]
        self.g[0].wait_recv()
        self.g[4] = new(one, one, self.right, self.grest)
        self.g[2].wait_recv()
        self.g[5] = new(two, two, self.left, self.grest)

    def gather_end(self):
        arrive(self.gwhole, self.grest)


class Direct:
    def __init__(self, copies, pos, dev):
        self.copies, self.pos, self.dev = copies, pos, dev

    def group(self, step):
        return pl.ds(pl.multiple_of(self.base + lax.rem(self.pos + step, 4) * self.size, 8), self.size)

    def reduce_start(self, ref, base, size, slots):
        self.ref, self.base, self.size, self.slots = ref, base, size, slots
        self.sem = self.copies.semaphore()
        for i in (2, 1, 3):
            self.copies.new(ref.at[self.group(i)], slots.at[i - 1], self.dev(i), self.sem)

    def reduce_end(self, out):
        arrive(self.slots, self.sem)
        at = self.group(0)
        out[at, :] = (self.ref[at, :] + self.slots[0]) + (self.slots[1] + self.slots[2])

    def gather_start(self, ref):
        own = ref.at[self.group(0)]
        self.sem = self.copies.semaphore()
        for i in (2, 1, 3):
            self.copies.new(own, own, self.dev(i), self.sem)

    def gather_end(self):
        arrive(self.slots, self.sem)


def dion_kernel(
    grad_hbm, mom_hbm, basis_hbm,
    nm_ref, nb_ref, uh, ul, inv_ref,
    grad, mom, bh, bl, qh, ql,
    pacc, pother, pown, precv, pslots, pfull, ph, plo,
    prow, gpart, gsum, gslots1, gslots2, gslots3, gmat, mat, tile, cols,
    zpart, zslots1, zslots2, zfull, lh, ll, squares, sqslots,
    load_sem, send_sem, recv_sem,
):
    f, t = lax.axis_index("fsdp"), lax.axis_index("tp")
    z, x, y, c = f // 4, f % 4, t // 2, t % 2

    def zdev(step):
        return (lax.rem(z + step, 4) * 4 + x, t)

    def xdev(step):
        return (z * 4 + lax.rem(x + step, 4), t)

    def ydev(step):
        return (f, lax.rem(y + step, 4) * 2 + c)

    def tdev(step):
        return (f, lax.rem(t + step, 8))

    sibling = (f, y * 2 + 1 - c)

    barrier = pltpu.get_barrier_semaphore()
    peers = [zdev(i) for i in (1, 2, 3)] + [xdev(i) for i in (1, 2, 3)] + [tdev(i) for i in range(1, 8)]
    for peer in peers:
        pl.semaphore_signal(barrier, inc=1, device_id=peer, device_id_type=MESH)

    def load(k):
        at = pl.ds(k * CHUNK, CHUNK)
        pltpu.make_async_copy(mom_hbm.at[:, at], mom.at[:, at], load_sem.at[k]).start()
        pltpu.make_async_copy(grad_hbm.at[:, at], grad.at[:, at], load_sem.at[k]).start()
        for half in range(2):
            pltpu.make_async_copy(
                basis_hbm.at[at, pl.ds(half * HALF, HALF)], zfull.at[half, at], load_sem.at[k]
            ).start()

    for k in range(CHUNKS):
        load(k)
    loaded = zpart.at[0, 0:1280]

    copies = Copies(send_sem, recv_sem)

    def partial(q, k):
        at = slice(k * CHUNK, k * CHUNK + CHUNK)
        columns = slice(q * HALF, q * HALF + HALF)
        term = dot3((bh[:, at], bl[:, at]), (qh[at, columns], ql[at, columns]))
        pacc[q] = term if k == 0 else pacc[q] + term

    def swap_start(q):
        pother[q] = pacc[q, :, pl.ds(pl.multiple_of((1 - c) * 128, 128), 128)]
        return copies.new(pother.at[q], precv.at[q], sibling)

    yring = [Ring(copies, y, ydev(1), ydev(3)) for _ in range(2)]

    def yrs_start(q):
        swaps[q].wait_recv()
        pown[q] = pacc[q, :, pl.ds(pl.multiple_of(c * 128, 128), 128)] + precv[q]
        yring[q].reduce_start(pown.at[q], 0, 128, pslots.at[q])
        yring[q].reduce_plain()

    shared = [[copies.semaphore() for _ in range(2)] for _ in range(2)]

    def share(q, step, semaphore):
        part = pfull.at[q, c, pl.ds(pl.multiple_of(lax.rem(y + step, 4) * 128, 128), 128)]
        copies.new(part, part, sibling, semaphore)

    def yrs_end(q):
        yring[q].reduce_end(pfull.at[q, c])
        yring[q].gather_start(pfull.at[q, c], 0, 128)
        share(q, 0, shared[q][0])

    def yag_end(q):
        yring[q].gather_end()
        for step in (1, 2, 3):
            share(q, step, shared[q][1])

    for k in range(CHUNKS):
        at = slice(k * CHUNK, k * CHUNK + CHUNK)
        arrive(loaded, load_sem.at[k])
        bh[:, at], bl[:, at] = split(mom[:, at] + grad[:, at].astype(f32))
        for half in range(2):
            columns = slice(half * HALF, half * HALF + HALF)
            qh[at, columns], ql[at, columns] = split(zfull[half, at, :])
        partial(0, k)
    pl.semaphore_wait(barrier, len(peers))
    swaps = [swap_start(0)]
    for k in range(CHUNKS):
        partial(1, k)
    swaps.append(swap_start(1))
    yrs_start(0)
    yrs_start(1)
    yring[0].reduce_middle()
    yring[1].reduce_middle()
    yrs_end(0)
    yrs_end(1)

    own_rows = pl.ds(pl.multiple_of(y * 128, 128), 128)
    for q in range(2):
        arrive(precv.at[q, 0:128], shared[q][0])
        for j in range(2):
            prow[:, q * HALF + j * 128 : q * HALF + j * 128 + 128] = pfull[q, j, own_rows, :]
    block = lambda i, width=1: prow[:, pl.ds(pl.multiple_of(i * 128, 128), width * 128)]
    over = ((0,), (0,))
    gpart[:, 0:384] = dot(block(c), block(c, 3), over, HIGHEST)
    gpart[:, 384:512] = dot(block(2 * c), block(3 - c), over, HIGHEST)
    gpart[:, 512:640] = dot(block(3 - c), block(3), over, HIGHEST)
    parts = (pl.ds(0, 384), pl.ds(384, 256))
    axes = ((z, zdev), (x, xdev))

    def rows(pos, step, size, base=0):
        return pl.ds(pl.multiple_of(base + lax.rem(pos + step, 4) * size, 8), size)

    def gram_send(stage):
        semaphore = copies.semaphore()
        for step in (1, 2, 3):
            for g in range(2):
                (pos, dev), (pos2, dev2) = axes[g], axes[1 - g]
                if stage == 1:
                    src, dst, to = gpart.at[rows(pos, step, 32), parts[g]], gslots1.at[step - 1, :, parts[g]], dev(step)
                elif stage == 2:
                    at = rows(pos2, step, 8, pos * 32)
                    src, dst, to = gsum.at[at, parts[g]], gslots2.at[step - 1, :, parts[g]], dev2(step)
                elif stage == 3:
                    at = rows(pos2, 0, 8, pos * 32)
                    src, dst, to = gsum.at[at, parts[g]], gslots3.at[step - 1, :, parts[g]], ydev(step)
                elif stage == 4:
                    at = rows(pos2, 0, 8, pos * 32)
                    src, dst, to = gmat.at[c, at, parts[g]], gmat.at[c, at, parts[g]], dev2(step)
                else:
                    at = rows(pos, 0, 32)
                    src, dst, to = gmat.at[c, at, parts[g]], gmat.at[c, at, parts[g]], dev(step)
                copies.new(src, dst, to, semaphore)
        return semaphore

    def gram_wait(stage, sent):
        arrive({1: gslots1, 2: gslots2, 3: gslots3, 4: gslots3, 5: gslots1}[stage], sent)
        if stage > 3:
            return
        for g in range(2):
            pos, pos2 = axes[g][0], axes[1 - g][0]
            if stage == 1:
                at = rows(pos, 0, 32)
                own, slots, out = gpart[at, parts[g]], gslots1, gsum
            elif stage == 2:
                at = rows(pos2, 0, 8, pos * 32)
                own, slots, out = gsum[at, parts[g]], gslots2, gsum
            else:
                at = rows(pos2, 0, 8, pos * 32)
                own, slots, out = gsum[at, parts[g]], gslots3, gmat.at[c]
            out[at, parts[g]] = (own + slots[0, :, parts[g]]) + (slots[1, :, parts[g]] + slots[2, :, parts[g]])

    sent = gram_send(1)
    yring[0].gather_middle()
    yring[1].gather_middle()
    yag_end(0)

    def product(q):
        arrive(precv.at[q, 0:384], shared[q][1])
        for j in range(2):
            ph[q, :, j * 128 : j * 128 + 128], plo[q, :, j * 128 : j * 128 + 128] = split(pfull[q, j])
        for k in range(CHUNKS):
            at = slice(k * CHUNK, k * CHUNK + CHUNK)
            zpart[q, at, :] = dot3((bh[:, at], bl[:, at]), (ph[q], plo[q]), ((0,), (0,)))

    tall = COL // 8
    short = tall // 4
    starts = (0, COL // 2)
    bases = (z * tall, COL // 2 + x * tall)
    first = [[Ring(copies, z, zdev(1), zdev(3)), Ring(copies, x, xdev(1), xdev(3))] for _ in range(2)]
    second = [[Direct(copies, x, xdev), Direct(copies, z, zdev)] for _ in range(2)]

    def rs1_start(q):
        for g in range(2):
            first[q][g].reduce_start(zpart.at[q], starts[g], tall, zslots1.at[q, g])
        for g in range(2):
            first[q][g].reduce_plain()

    def rs1_middle(q):
        for g in range(2):
            first[q][g].reduce_middle()

    def rs1_end(q):
        for g in range(2):
            first[q][g].reduce_end(zpart.at[q])
            second[q][g].reduce_start(zpart.at[q], bases[g], short, zslots2.at[q, g])

    def rs2_end(q):
        for g in range(2):
            second[q][g].reduce_end(zfull.at[q])
            second[q][g].gather_start(zfull.at[q])

    def ag1_end(q):
        for g in range(2):
            second[q][g].gather_end()
            first[q][g].gather_start(zfull.at[q], starts[g], tall)

    def ag2_middle(q):
        for g in range(2):
            first[q][g].gather_middle()

    def ag2_end(q):
        for g in range(2):
            first[q][g].gather_end()

    gram_wait(1, sent)
    sent = gram_send(2)
    product(0)
    gram_wait(2, sent)
    sent = gram_send(3)
    rs1_start(0)
    sums_sent = copies.count()
    yag_end(1)
    product(1)
    copies.drain(sums_sent - 20)
    gram_wait(3, sent)
    sent = gram_send(4)
    rs1_middle(0)
    gram_wait(4, sent)
    sent = gram_send(5)
    rs1_start(1)
    first_sent = copies.count()
    rs1_end(0)
    gram_wait(5, sent)
    swap = copies.new(gmat.at[c], gmat.at[c], sibling)
    rs1_middle(1)
    swap.wait_recv()
    for i, g, first_block, width, where in (
        (0, 0, 0, 3, 0), (0, 0, 3, 1, 384), (3, 0, 3, 1, 512),
        (1, 1, 1, 3, 0), (2, 1, 2, 1, 384), (2, 1, 3, 1, 512),
    ):
        mat[i * 128 : i * 128 + 128, first_block * 128 : (first_block + width) * 128] = gmat[
            g, :, where : where + width * 128
        ]

    work = factor(mat, tile, cols)

    def steps(n):
        for _ in range(n):
            next(work)

    steps(1)
    rs2_end(0)
    steps(2)
    rs1_end(1)
    steps(2)
    ag1_end(0)
    copies.drain(first_sent)
    steps(3)
    rs2_end(1)
    steps(3)
    ag2_middle(0)
    ag1_end(1)
    most_sent = copies.count() - 16
    steps(6)
    ag2_middle(1)
    steps(3)
    r = lax.broadcasted_iota(jnp.int32, (RANK, RANK), 0)
    k = lax.broadcasted_iota(jnp.int32, (RANK, RANK), 1)
    lh[...], ll[...] = split(jnp.where(r >= k, mat[...], 0.0))
    last = ((1,), (1,))

    def solve(pairs):
        low, high = slice(0, HALF), slice(HALF, RANK)
        factor_of = lambda rows_, columns: (lh[rows_, columns], ll[rows_, columns])
        left = dot3(pairs[0], factor_of(low, low), last)
        right = dot3(pairs[0], factor_of(high, low), last) + dot3(pairs[1], factor_of(high, high), last)
        return left, right

    shard = [
        jnp.concatenate([zfull[q, second[q][g].group(0), :] for g in range(2)], axis=0) for q in range(2)
    ]
    for q, w in enumerate(solve([split(part) for part in shard])):
        squares[0, :, q * HALF : q * HALF + HALF] = jnp.sum((w * w).reshape(short // 4, 8, HALF), axis=0)

    def norm_send(stage):
        steps_, dev = ((1, 2, 3), zdev) if stage == 0 else ((1, 2, 3), xdev) if stage == 1 else (range(1, 8), tdev)
        semaphore = copies.semaphore()
        for i in steps_:
            copies.new(squares.at[stage], sqslots.at[stage, i - 1], dev(i), semaphore)
        return semaphore

    def norm_wait(stage, sent):
        total = squares[stage]
        number = 7 if stage == 2 else 3
        arrive(sqslots.at[stage, 0:number], sent)
        for i in range(number):
            total = total + sqslots[stage, i]
        squares[stage + 1] = total

    sent = norm_send(0)
    for q, u in enumerate(solve([(ph[half], plo[half]) for half in range(2)])):
        at = slice(q * HALF, q * HALF + HALF)
        uh[:, at], ul[:, at] = split(u)

    low, high = slice(0, HALF), slice(HALF, RANK)

    def early(k):
        at = slice(k * CHUNK, k * CHUNK + CHUNK)
        part = split(zfull[0, at, :])
        nb_ref[at, low] = dot3(part, (lh[low, low], ll[low, low]), last)
        nb_ref[at, high] = dot3(part, (lh[high, low], ll[high, low]), last)

    def back(k):
        at = slice(k * CHUNK, k * CHUNK + CHUNK)
        nb_ref[at, high] = nb_ref[at, high] + dot3(split(zfull[1, at, :]), (lh[high, high], ll[high, high]), last)
        update = dot(uh[...], nb_ref[at, :].astype(bf16), last)
        nm_ref[:, at] = (mom[:, at] + grad[:, at].astype(f32)) - 0.05 * update

    ag2_end(0)
    norm_wait(0, sent)
    sent = norm_send(1)
    for i in range(4):
        early(i)
    norm_wait(1, sent)
    sent = norm_send(2)
    for i in range(4, CHUNKS):
        early(i)
    copies.drain(most_sent)
    ag2_end(1)
    for i in range(CHUNKS):
        back(i)
    norm_wait(2, sent)
    norms = jnp.sqrt(jnp.sum(squares[3], axis=0, keepdims=True))
    inv_ref[...] = jnp.broadcast_to(1.0 / (norms + 1e-08), (8, RANK))
    copies.drain(copies.count())


def finish_kernel(scale, nm, w, uh, ul, inv, nm_out, nb_out, up_out, nb, up, sem):
    pltpu.make_async_copy(nm, nm_out, sem.at[0]).start()
    for k in range(CHUNKS):
        at = slice(k * CHUNK, k * CHUNK + CHUNK)
        n = w[at, :] * inv[0:1, :]
        nb[at, :] = n
        pltpu.make_async_copy(nb.at[at, :], nb_out.at[at, :], sem.at[1]).start()
        up[:, at] = (scale * dot3((uh[...], ul[...]), split(n), ((1,), (1,)))).astype(bf16)
        pltpu.make_async_copy(up.at[:, at], up_out.at[:, at], sem.at[2]).start()
    for i, (src, dst) in enumerate(((nm, nm_out), (nb, nb_out), (up, up_out))):
        pltpu.make_async_copy(src, dst, sem.at[i]).wait()


SENDS = 78
ARRIVALS = 59


def local(gradient, momentum, basis):
    vmem = lambda shape, kind=f32: pltpu.VMEM(shape, kind)
    shapes = [
        jax.ShapeDtypeStruct((ROW, COL), f32),
        jax.ShapeDtypeStruct((COL, RANK), f32),
        jax.ShapeDtypeStruct((ROW, COL), bf16),
    ]
    results = pl.pallas_call(
        dion_kernel,
        out_shape=shapes[:2] + [
            jax.ShapeDtypeStruct((ROW, RANK), bf16),
            jax.ShapeDtypeStruct((ROW, RANK), bf16),
            jax.ShapeDtypeStruct((8, RANK), f32),
        ],
        in_specs=[pl.BlockSpec(memory_space=pltpu.HBM)] * 3,
        out_specs=[pl.BlockSpec(memory_space=pltpu.VMEM)] * 5,
        scratch_shapes=[
            vmem((ROW, COL), bf16), vmem((ROW, COL)),
            vmem((ROW, COL), bf16), vmem((ROW, COL), bf16),
            vmem((COL, RANK), bf16), vmem((COL, RANK), bf16),
            vmem((2, ROW, HALF)), vmem((2, ROW, 128)), vmem((2, ROW, 128)), vmem((2, ROW, 128)),
            vmem((2, 6, 64, 128)), vmem((2, 2, ROW, 128)),
            vmem((2, ROW, HALF), bf16), vmem((2, ROW, HALF), bf16),
            vmem((128, RANK)), vmem((128, 640)), vmem((128, 640)),
            vmem((3, 32, 640)), vmem((3, 8, 640)), vmem((3, 8, 640)), vmem((2, 128, 640)), vmem((RANK, RANK)),
            vmem((128, 256)), vmem((64, 128)),
            vmem((2, COL, HALF)), vmem((2, 2, 6, COL // 16, HALF)), vmem((2, 2, 3, COL // 32, HALF)),
            vmem((2, COL, HALF)),
            vmem((RANK, RANK), bf16), vmem((RANK, RANK), bf16),
            vmem((4, 8, RANK)), vmem((3, 7, 8, RANK)),
            pltpu.SemaphoreType.DMA((CHUNKS,)),
            pltpu.SemaphoreType.DMA((SENDS,)),
            pltpu.SemaphoreType.DMA((ARRIVALS,)),
        ],
        compiler_params=pltpu.CompilerParams(
            collective_id=0, has_side_effects=True, vmem_limit_bytes=40 << 20
        ),
        name="dion",
    )(*(pltpu.with_memory_space_constraint(a, pltpu.HBM) for a in (gradient, momentum, basis)))
    return tuple(pl.pallas_call(
        functools.partial(finish_kernel, float((ROWS * COLS / RANK) ** 0.5)),
        out_shape=shapes,
        in_specs=[pl.BlockSpec(memory_space=pltpu.VMEM)] * 5,
        out_specs=[pl.BlockSpec(memory_space=pltpu.HBM)] * 3,
        scratch_shapes=[vmem((COL, RANK)), vmem((ROW, COL), bf16), pltpu.SemaphoreType.DMA((3,))],
        compiler_params=pltpu.CompilerParams(vmem_limit_bytes=10 << 20),
        name="finish",
    )(*results))


def solution(mesh):
    return jax.shard_map(
        local,
        mesh=mesh,
        in_specs=(P("fsdp", "tp"), P("fsdp", "tp"), P("tp", None)),
        out_specs=(P("fsdp", "tp"), P("tp", None), P("fsdp", "tp")),
        check_vma=False,
    )
```

time: 497 us -> 94.1 us (0.19); the launches traced: 491 us -> 94 us
  waiting for transfers between devices: 250 us -> 0 us
  other arithmetic: 127 us -> 0 us
  Pallas kernels: 0 us -> 93.2 us
  matrix products: 68 us -> 0 us
  local copies, waits for them, and re-layouts: 16.1 us -> 0 us
  between operations: 16.8 us -> 0.82 us
  blocking collectives: 12.8 us -> 0 us
    psum x3 -> x0, waiting for transfers between devices: 250 us -> none  [the longest x1 99.5 us: local(): back = lax.psum(inner(buffer, ortho), 'fsdp')]
    another operation x17 -> x0, other arithmetic: 120 us -> none  [the longest x14 78.8 us: orthonormal(): lower = jnp.linalg.cholesky(gram)]
    pallas_call x0 -> x2, Pallas kernels: none -> 93.2 us  [the longest x1 89 us: local(): pl.pallas_call(dion_kernel, out_shape=shapes[:2] + [jax.ShapeDtypeStruct(...]
    dot_general x5 -> x0, matrix products: 55.6 us -> none  [the longest x2 27 us: outer(): lax.dot_general(left, right, (((1,), (1,)), ((), ())), precision=lax.Prec...]
    another operation x17 -> x0, local copies, waits for them, and re-layouts: 14.3 us -> none
    psum x1 -> x0, blocking collectives: 12.8 us -> none  [local(): squares = lax.psum(jnp.sum(back * back, axis=0), 'tp')]
    another operation x13 -> x0, matrix products: 12.4 us -> none  [the longest x7 10.5 us: orthonormal(): return jax.scipy.linalg.solve_triangular(lower, projected.T, lower=True).T]
  transfers between devices with their start and end apart: 3 -> 0, of which waited for: 3 -> 0; matrix products, arithmetic and copies ran while one was open for 0% -> 0% of each run, Pallas kernels for 0% -> 0%
where the time goes in v2:
time: 94.1 us; the launch traced here: 94 us
  Pallas kernels  93.2 us (99%)
    pallas_call x1, Pallas kernels, local(): pl.pallas_call(dion_kernel, out_shape=shapes[:2] + [jax.ShapeDtypeStruct(...  89 us
    pallas_call x1, Pallas kernels, local(): pl.pallas_call(functools.partial(finish_kernel, float((ROWS * COLS / RANK...  4.24 us

profile of v2, /device:TPU:1, one launch (start us, length us, event | category | flops | bytes accessed | tf_op | source)
XLA Modules:
  0.0 94.0 jit_solution(14297975314389900736)
XLA Ops:
  0.6 89.0 %dion.1 = (f32[512,1792]{1,0:T(8,128)S(1)}, f32[1792,512]{1,0:T(8,128)S(1)}, bf16[512,512]{1,0:T(8,128)(2,1)S(1)}, bf16[512,512]{1,0:T(8,128)(2,1)S(1)}, f32[8,512]{1,0:T(8,128)S(1)}) custom-call(bf16[512,1792]{1,0:T(8,128)(2,1)} %grad_hbm.1, f32[512,1792]{1,0:T(8,128)} %mom_hbm.1, f32[1792,512]{1,0:T(8,128)} %basis_hbm.1), custom_call_target="tpu_custom_call" | custom-call | tf_op jit(solution)/shard_map/dion/pallas_call | solution.py:596
  89.6 4.2 %finish.1 = (f32[512,1792]{1,0:T(8,128)}, f32[1792,512]{1,0:T(8,128)}, bf16[512,1792]{1,0:T(8,128)(2,1)}) custom-call(f32[512,1792]{1,0:T(8,128)S(1)} %get-tuple-element.8.nm, f32[1792,512]{1,0:T(8,128)S(1)} %get-tuple-element.9.w, bf16[512,512]{1,0:T(8,128)(2,1)S(1)} %get-tuple-element.10.uh, bf16[512,512]{1,0:T(8,128)(2,1)S(1)} %get-tuple-element.11.ul, ...), custom_call_target="tpu_custom_call" | custom-call | tf_op jit(solution)/shard_map/finish/pallas_call | solution.py:628

commit v3 on v2

--- a/solution.py
+++ b/solution.py
@@ -195,6 +195,10 @@
         self.grest, self.gwhole = self.copies.semaphore(), ref.at[pl.ds(base, 2 * size)]
         self.g[0] = new(one, one, self.right)
         self.g[2] = new(two, two, self.left)
+
+    def gather_rest(self):
+        new, ref, at = self.copies.new, self.out, self.gat
+        one, two = ref.at[at(0, 0)], ref.at[at(0, 1)]
         self.g[1] = new(two, two, self.right, self.grest)
         self.g[3] = new(one, one, self.left, self.grest)
 
@@ -311,6 +315,7 @@
     def yrs_end(q):
         yring[q].reduce_end(pfull.at[q, c])
         yring[q].gather_start(pfull.at[q, c], 0, 128)
+        yring[q].gather_rest()
         share(q, 0, shared[q][0])
 
     def yag_end(q):
@@ -438,6 +443,10 @@
             second[q][g].gather_end()
             first[q][g].gather_start(zfull.at[q], starts[g], tall)
 
+    def ag2_rest(q):
+        for g in range(2):
+            first[q][g].gather_rest()
+
     def ag2_middle(q):
         for g in range(2):
             first[q][g].gather_middle()
@@ -466,7 +475,6 @@
     rs1_end(0)
     gram_wait(5, sent)
     swap = copies.new(gmat.at[c], gmat.at[c], sibling)
-    rs1_middle(1)
     swap.wait_recv()
     for i, g, first_block, width, where in (
         (0, 0, 0, 3, 0), (0, 0, 3, 1, 384), (3, 0, 3, 1, 512),
@@ -482,22 +490,21 @@
         for _ in range(n):
             next(work)
 
-    steps(1)
+    steps(2)
+    rs1_middle(1)
+    steps(4)
     rs2_end(0)
-    steps(2)
+    steps(3)
     rs1_end(1)
     steps(2)
     ag1_end(0)
-    copies.drain(first_sent)
     steps(3)
     rs2_end(1)
-    steps(3)
+    ag2_rest(0)
+    copies.drain(first_sent)
+    steps(4)
     ag2_middle(0)
-    ag1_end(1)
-    most_sent = copies.count() - 16
-    steps(6)
-    ag2_middle(1)
-    steps(3)
+    steps(2)
     r = lax.broadcasted_iota(jnp.int32, (RANK, RANK), 0)
     k = lax.broadcasted_iota(jnp.int32, (RANK, RANK), 1)
     lh[...], ll[...] = split(jnp.where(r >= k, mat[...], 0.0))
@@ -532,6 +539,7 @@
         squares[stage + 1] = total
 
     sent = norm_send(0)
+    ag1_end(1)
     for q, u in enumerate(solve([(ph[half], plo[half]) for half in range(2)])):
         at = slice(q * HALF, q * HALF + HALF)
         uh[:, at], ul[:, at] = split(u)
@@ -550,14 +558,17 @@
         update = dot(uh[...], nb_ref[at, :].astype(bf16), last)
         nm_ref[:, at] = (mom[:, at] + grad[:, at].astype(f32)) - 0.05 * update
 
-    ag2_end(0)
+    ag2_rest(1)
+    most_sent = copies.count() - 16
     norm_wait(0, sent)
     sent = norm_send(1)
-    for i in range(4):
+    ag2_end(0)
+    for i in range(3):
         early(i)
+    ag2_middle(1)
     norm_wait(1, sent)
     sent = norm_send(2)
-    for i in range(4, CHUNKS):
+    for i in range(3, CHUNKS):
         early(i)
     copies.drain(most_sent)
     ag2_end(1)
@@ -582,7 +593,7 @@
         pltpu.make_async_copy(src, dst, sem.at[i]).wait()
 
 
-SENDS = 78
+SENDS = 84
 ARRIVALS = 59
 
 

time: 94.1 us -> 87.8 us (0.933)
  Pallas kernels: 93.2 us -> 86.8 us
    pallas_call x1, Pallas kernels: 89 us -> 82.6 us  [local(): pl.pallas_call(dion_kernel, out_shape=shapes[:2] + [jax.ShapeDtypeStruct(...]
where the time goes in v3:
time: 87.8 us; the launch traced here: 87.7 us
  Pallas kernels  86.8 us (99%)
    pallas_call x1, Pallas kernels, local(): pl.pallas_call(dion_kernel, out_shape=shapes[:2] + [jax.ShapeDtypeStruct(...  82.6 us
    pallas_call x1, Pallas kernels, local(): pl.pallas_call(functools.partial(finish_kernel, float((ROWS * COLS / RANK...  4.24 us

profile of v3, /device:TPU:1, one launch (start us, length us, event | category | flops | bytes accessed | tf_op | source)
XLA Modules:
  0.0 87.7 jit_solution(3689755337103787117)
XLA Ops:
  0.6 82.6 %dion.1 = (f32[512,1792]{1,0:T(8,128)S(1)}, f32[1792,512]{1,0:T(8,128)S(1)}, bf16[512,512]{1,0:T(8,128)(2,1)S(1)}, bf16[512,512]{1,0:T(8,128)(2,1)S(1)}, f32[8,512]{1,0:T(8,128)S(1)}) custom-call(bf16[512,1792]{1,0:T(8,128)(2,1)} %grad_hbm.1, f32[512,1792]{1,0:T(8,128)} %mom_hbm.1, f32[1792,512]{1,0:T(8,128)} %basis_hbm.1), custom_call_target="tpu_custom_call" | custom-call | tf_op jit(solution)/shard_map/dion/pallas_call | solution.py:607
  83.2 4.2 %finish.1 = (f32[512,1792]{1,0:T(8,128)}, f32[1792,512]{1,0:T(8,128)}, bf16[512,1792]{1,0:T(8,128)(2,1)}) custom-call(f32[512,1792]{1,0:T(8,128)S(1)} %get-tuple-element.8.nm, f32[1792,512]{1,0:T(8,128)S(1)} %get-tuple-element.9.w, bf16[512,512]{1,0:T(8,128)(2,1)S(1)} %get-tuple-element.10.uh, bf16[512,512]{1,0:T(8,128)(2,1)S(1)} %get-tuple-element.11.ul, ...), custom_call_target="tpu_custom_call" | custom-call | tf_op jit(solution)/shard_map/finish/pallas_call | solution.py:639

commit v4 on v3

--- a/solution.py
+++ b/solution.py
@@ -540,6 +540,7 @@
 
     sent = norm_send(0)
     ag1_end(1)
+    ag2_rest(1)
     for q, u in enumerate(solve([(ph[half], plo[half]) for half in range(2)])):
         at = slice(q * HALF, q * HALF + HALF)
         uh[:, at], ul[:, at] = split(u)
@@ -558,7 +559,6 @@
         update = dot(uh[...], nb_ref[at, :].astype(bf16), last)
         nm_ref[:, at] = (mom[:, at] + grad[:, at].astype(f32)) - 0.05 * update
 
-    ag2_rest(1)
     most_sent = copies.count() - 16
     norm_wait(0, sent)
     sent = norm_send(1)

time: 87.8 us -> 87.8 us (level)
  no operation moved by 1% of the time
where the time goes in v4:
time: 87.8 us; the launch traced here: 87.7 us
  Pallas kernels  86.8 us (99%)
    pallas_call x1, Pallas kernels, local(): pl.pallas_call(dion_kernel, out_shape=shapes[:2] + [jax.ShapeDtypeStruct(...  82.6 us
    pallas_call x1, Pallas kernels, local(): pl.pallas_call(functools.partial(finish_kernel, float((ROWS * COLS / RANK...  4.24 us

profile of v4, /device:TPU:1, one launch (start us, length us, event | category | flops | bytes accessed | tf_op | source)
XLA Modules:
  0.0 87.7 jit_solution(9990830121999220026)
XLA Ops:
  0.6 82.6 %dion.1 = (f32[512,1792]{1,0:T(8,128)S(1)}, f32[1792,512]{1,0:T(8,128)S(1)}, bf16[512,512]{1,0:T(8,128)(2,1)S(1)}, bf16[512,512]{1,0:T(8,128)(2,1)S(1)}, f32[8,512]{1,0:T(8,128)S(1)}) custom-call(bf16[512,1792]{1,0:T(8,128)(2,1)} %grad_hbm.1, f32[512,1792]{1,0:T(8,128)} %mom_hbm.1, f32[1792,512]{1,0:T(8,128)} %basis_hbm.1), custom_call_target="tpu_custom_call" | custom-call | tf_op jit(solution)/shard_map/dion/pallas_call | solution.py:607
  83.2 4.2 %finish.1 = (f32[512,1792]{1,0:T(8,128)}, f32[1792,512]{1,0:T(8,128)}, bf16[512,1792]{1,0:T(8,128)(2,1)}) custom-call(f32[512,1792]{1,0:T(8,128)S(1)} %get-tuple-element.8.nm, f32[1792,512]{1,0:T(8,128)S(1)} %get-tuple-element.9.w, bf16[512,512]{1,0:T(8,128)(2,1)S(1)} %get-tuple-element.10.uh, bf16[512,512]{1,0:T(8,128)(2,1)S(1)} %get-tuple-element.11.ul, ...), custom_call_target="tpu_custom_call" | custom-call | tf_op jit(solution)/shard_map/finish/pallas_call | solution.py:639
